TPU v7x, 256 devices: a whole 4x4x8 slice. The times are simulated.
256 devices in a mesh: chan: 32 (over z, x), tm: 8 (over y, core).
Axes of the slice: x: 4, y: 4, z: 8, core: 2. Of those that a mesh axis runs over, the one named last changes fastest.
Arguments:
- solution: float32 [2, 8, 1024, 8192], P(None, None, 'chan', 'tm'), may hold values from -6 to 6
- residual: float32 [2, 8, 1024, 8192], P(None, None, 'chan', 'tm'), may hold values from -80 to 80
- direction: float32 [2, 8, 1024, 8192], P(None, None, 'chan', 'tm'), may hold values from -80 to 80
- sample_weight: float32 [8, 32, 32, 2048], P('tm', 'chan'), may hold values from 0.15 to 3
Outputs:
- new_solution: float32 [2, 8, 1024, 8192], P(None, None, 'chan', 'tm')
- new_residual: float32 [2, 8, 1024, 8192], P(None, None, 'chan', 'tm')
- new_direction: float32 [2, 8, 1024, 8192], P(None, None, 'chan', 'tm')
All inputs are finite; a program needn't handle non-finite values.
Results may differ from a plain program's by a relative error of at most 0.00012.
Values sent between devices are 32-bit elements; how exact they have to be, the bound alone decides.
A program may use at most 128 MiB of HBM per device.

v0:
```python
import math

import jax
import jax.numpy as jnp
from jax import lax
from jax.sharding import PartitionSpec as P

SAMPLES = 2048
CHANNELS = 1024
TAPS = 4


def shifted(block, axis, distance):
    devices = range(lax.axis_size(axis))
    route = [((i - distance) % len(devices), i) for i in devices]
    return lax.ppermute(block, axis, route)


def passed_along(block, axis, distance):
    devices = range(lax.axis_size(axis))
    route = [(i - distance, i) for i in devices if i - distance in devices]
    return lax.ppermute(block, axis, route)


def pfb_window():
    position = jnp.arange(TAPS * SAMPLES, dtype=jnp.float32)
    taper = 0.5 - 0.5 * jnp.cos(2.0 * math.pi * position / (TAPS * SAMPLES - 1))
    return (jnp.sinc(position / SAMPLES - TAPS / 2) * taper).reshape(TAPS, SAMPLES)


def dense_table():
    chan_index = jnp.arange(CHANNELS, dtype=jnp.int32)[:, None]
    sample_index = jnp.arange(SAMPLES, dtype=jnp.int32)[None, :]
    phase = (chan_index * sample_index % SAMPLES).astype(jnp.float32)
    angle = 2.0 * math.pi / SAMPLES * phase
    return jnp.stack([jnp.cos(angle), -jnp.sin(angle)]) / math.sqrt(SAMPLES)


def to_spectra(weighted, tables):
    return jnp.einsum("fmn,ckn->cfkm", weighted, tables, precision=lax.Precision.HIGHEST)


def to_samples(spectra, tables):
    return jnp.einsum("cfkm,ckn->fmn", spectra, tables, precision=lax.Precision.HIGHEST)


def per_device(solution, residual, direction, sample_weight):
    window = pfb_window()
    tables = dense_table()
    rim = TAPS - 1
    group_count = lax.axis_size("chan")
    lead, feeds_here, chans_here, frames_here = direction.shape
    block_len = frames_here // group_count
    noise = sample_weight.reshape(sample_weight.shape[2], sample_weight.shape[3])
    first_block = lax.axis_index("chan") == 0
    last_block = lax.axis_index("chan") == group_count - 1
    norm_now = lax.psum(jnp.sum(residual * residual), ("chan", "tm"))
    sectioned = direction.reshape(lead, feeds_here, chans_here, group_count, block_len)
    spectra = lax.all_to_all(sectioned, "chan", split_axis=3, concat_axis=2, tiled=True)
    spectra = spectra[:, :, :, 0, :]
    samples = to_samples(spectra, tables)
    moved = shifted(samples[:, block_len - rim :, :], "chan", 1)
    carried = passed_along(moved, "tm", 1)
    from_below = jnp.where(first_block, carried, moved)
    extended = jnp.concatenate([from_below, samples], axis=1)
    adjoint = jnp.zeros_like(samples)
    for tap_index in range(TAPS):
        adjoint = (
            adjoint
            + window[tap_index] * extended[:, rim - tap_index : rim - tap_index + block_len, :]
        )
    stream = noise[None] * adjoint
    moved_up = shifted(stream[:, :rim, :], "chan", -1)
    carried_up = passed_along(moved_up, "tm", -1)
    from_above = jnp.where(last_block, carried_up, moved_up)
    widened = jnp.concatenate([stream, from_above], axis=1)
    weighted = jnp.zeros_like(stream)
    for tap_index in range(TAPS):
        weighted = weighted + window[tap_index] * widened[:, tap_index : tap_index + block_len, :]
    framed = to_spectra(weighted, tables)[:, :, :, None, :]
    image = lax.all_to_all(framed, "chan", split_axis=2, concat_axis=3, tiled=True).reshape(
        direction.shape
    )
    curvature = lax.psum(jnp.sum(direction * image), ("chan", "tm"))
    alpha = norm_now / curvature
    new_residual = residual - alpha * image
    norm_next = lax.psum(jnp.sum(new_residual * new_residual), ("chan", "tm"))
    new_solution = solution + alpha * direction
    new_direction = new_residual + norm_next / norm_now * direction
    return (new_solution, new_residual, new_direction)


def solution(mesh):
    placed = (
        P(None, None, "chan", "tm"),
        P(None, None, "chan", "tm"),
        P(None, None, "chan", "tm"),
        P("tm", "chan", None, None),
    )
    return jax.shard_map(
        per_device,
        mesh=mesh,
        in_specs=placed,
        out_specs=(
            P(None, None, "chan", "tm"),
            P(None, None, "chan", "tm"),
            P(None, None, "chan", "tm"),
        ),
        check_vma=False,
    )
```

profile of v0, /device:TPU:1, one launch (start us, length us, event | category | flops | bytes accessed | tf_op | source)
XLA Modules:
  0.0 467.5 jit_solution(16830977813516249870)
XLA Ops:
  0.6 6.5 %reshape.99 = f32[2,8,32,32,32]{4,3,2,1,0:T(8,128)} reshape(f32[2,8,32,1024]{3,2,1,0:T(8,128)} %param.6) | data formatting | bytes 4194304 | tf_op jit(solution)/shard_map/reshape | solution.py:58
  7.1 9.6 %copy.12 = f32[2,8,32,32,32]{2,4,0,1,3:T(8,128)} copy(f32[2,8,32,32,32]{4,3,2,1,0:T(8,128)} %reshape.99) | data formatting | bytes 4194304 | tf_op jit(solution)/shard_map/reshape | solution.py:58
  16.7 7.7 %reshape.104 = f32[32,1,16384]{2,1,0:T(1,128)} reshape(f32[32,8,2,32,32]{4,3,2,1,0:T(8,128)} %bitcast.51) | data formatting | bytes 4194304
  24.4 11.9 %all-to-all-start = ((f32[32,1,16384]{2,1,0:T(1,128)}), f32[32,1,16384]{2,1,0:T(1,128)S(1)}, u32[]{:S(2)}, u32[]{:S(2)}) async-start(f32[32,1,16384]{2,1,0:T(1,128)} %reshape.104), calls=%async_computation | async-start | bytes 4194304 | tf_op jit(solution)/shard_map/all_to_all | solution.py:59
  36.3 34.6 %sine_negate_fusion = (f32[1,1024,2048]{2,1,0:T(8,128)}, f32[1,1024,2048]{2,1,0:T(8,128)}) fusion(), kind=kLoop, calls=%fused_computation.13 | loop fusion | flops 31457280 | bytes 16777216 | tf_op jit(solution)/shard_map/neg | solution.py:36
  70.9 13.9 %all-to-all-done = f32[32,1,16384]{2,1,0:T(1,128)S(1)} async-done(((f32[32,1,16384]{2,1,0:T(1,128)}), f32[32,1,16384]{2,1,0:T(1,128)S(1)}, u32[]{:S(2)}, u32[]{:S(2)}) %all-to-all-start) | async-done | bytes 2097184 | tf_op jit(solution)/shard_map/all_to_all | solution.py:59
  86.6 7.4 %reduce = f32[32,16384]{1,0:T(8,128)S(1)} reduce(f32[32,1,16384]{2,1,0:T(1,128)} %copy-done.1, f32[]{:T(128)} %broadcast.102), dimensions={1}, to_apply=%all_to_all.22.reduce_sub_computation | reduce | bytes 4194308 | tf_op jit(solution)/shard_map/all_to_all | solution.py:59
  94.0 5.0 %reshape.105 = f32[32,8,2,32,32]{4,3,2,1,0:T(8,128)} reshape(f32[32,16384]{1,0:T(8,128)S(1)} %reduce) | data formatting | bytes 4194304
  99.0 4.4 bitcast_bitcast_fusion
  103.4 9.7 %copy.13 = f32[2,8,32,32,1,32]{3,2,5,0,1,4:T(8,128)} copy(f32[2,8,32,32,1,32]{3,5,0,1,2,4:T(8,128)S(1)} %bitcast_bitcast_fusion) | data formatting | bytes 4194304 | tf_op jit(solution)/shard_map/all_to_all | solution.py:59
  113.2 7.7 %squeeze.3 = f32[2,8,1024,32]{2,3,0,1:T(8,128)} reshape(f32[2,8,32,32,1,32]{3,2,5,0,1,4:T(8,128)} %copy.13) | data formatting | bytes 4194304 | tf_op jit(solution)/shard_map/squeeze | solution.py:60
  120.9 18.9 %fusion.13 = f32[8,32,2048]{2,1,0:T(8,128)S(1)} fusion(f32[2,8,1024,32]{2,3,0,1:T(8,128)} %squeeze.3, f32[1,1024,2048]{2,1,0:T(8,128)} %get-tuple-element.13, f32[1,1024,2048]{2,1,0:T(8,128)} %get-tuple-element.14), kind=kOutput, calls=%fused_computation.22 | convolution fusion | flops 12893290496 | bytes 20971520 | tf_op jit(solution)/shard_map/cfkm,ckn->fmn/dot_general | solution.py:44
  139.8 2.1 collective-permute-start
  142.1 6.3 %collective-permute-done = f32[8,3,2048]{2,1,0:T(4,128)S(1)} collective-permute-done((f32[8,3,2048]{2,1,0:T(4,128)S(1)}, f32[8,3,2048]{2,1,0:T(4,128)S(1)}, u32[]{:S(2)}, u32[]{:S(2)}) %collective-permute-start) | collective-permute-done | bytes 196640 | tf_op jit(solution)/shard_map/ppermute | solution.py:16
  148.5 6.9 %collective-permute-start.1 = (f32[8,3,2048]{2,1,0:T(4,128)S(1)}, f32[8,3,2048]{2,1,0:T(4,128)S(1)}, u32[]{:S(2)}, u32[]{:S(2)}) collective-permute-start(f32[8,3,2048]{2,1,0:T(4,128)S(1)} %collective-permute-done), channel_id=1, source_target_pairs={{0,1},{1,2},{2,3},{3,4},{4,5},{5,6},{6,7},{8,9},{9,10},{10,11},{11... | collective-permute-start | bytes 589832 | tf_op jit(solution)/shard_map/ppermute | solution.py:22
  155.3 3.3 collective-permute-done.1
  161.3 5.2 %collective-permute-done.2 = f32[8,3,2048]{2,1,0:T(4,128)S(1)} collective-permute-done((f32[8,3,2048]{2,1,0:T(4,128)S(1)}, f32[8,3,2048]{2,1,0:T(4,128)S(1)}, u32[]{:S(2)}, u32[]{:S(2)}) %collective-permute-start.2) | collective-permute-done | bytes 196640 | tf_op jit(solution)/shard_map/ppermute | solution.py:16
  168.4 8.7 %collective-permute-done.3 = f32[8,3,2048]{2,1,0:T(4,128)S(1)} collective-permute-done((f32[8,3,2048]{2,1,0:T(4,128)S(1)}, f32[8,3,2048]{2,1,0:T(4,128)S(1)}, u32[]{:S(2)}, u32[]{:S(2)}) %collective-permute-start.3) | collective-permute-done | bytes 196640 | tf_op jit(solution)/shard_map/ppermute | solution.py:22
  177.2 26.6 %fusion.39 = f32[2,8,1024,1,32]{2,4,1,0,3:T(8,128)S(1)} fusion(f32[8,32,2048]{2,1,0:T(8,128)} %copy-done.2, f32[8,3,2048]{2,1,0:T(4,128)S(1)} %broadcast_select_fusion, f32[1,1024,2048]{2,1,0:T(8,128)} %get-tuple-element.13, f32[1,1024,2048]{2,1,0:T(8,128)} %get-tuple-element.14, f32[2048]{0:T(1024)S(1)} %get-tuple-element.10, ...), kind=kOutput, calls=%fused_computation.55 | convolution fusion | flops 12898533376 | bytes 21200896 | tf_op jit(solution)/shard_map/fmn,ckn->cfkm/dot_general | solution.py:40
  203.7 6.2 %copy.14 = f32[2,8,1024,1,32]{4,1,0,3,2:T(8,128)} copy(f32[2,8,1024,1,32]{2,4,1,0,3:T(8,128)S(1)} %fusion.39) | data formatting | bytes 4194304 | tf_op jit(solution)/shard_map/broadcast_in_dim | solution.py:80
  210.0 7.7 %reshape.106 = f32[32,1,16384]{2,1,0:T(1,128)} reshape(f32[1024,1,2,8,32]{4,3,2,1,0:T(8,128)} %bitcast.50) | data formatting | bytes 4194304
  217.7 5.8 %all-to-all-start.1 = ((f32[32,1,16384]{2,1,0:T(1,128)}), f32[32,1,16384]{2,1,0:T(1,128)}, u32[]{:S(2)}, u32[]{:S(2)}) async-start(f32[32,1,16384]{2,1,0:T(1,128)} %reshape.106), calls=%async_computation.1 | async-start | bytes 4194304 | tf_op jit(solution)/shard_map/all_to_all | solution.py:81
  224.7 42.8 %all-to-all-done.1 = f32[32,1,16384]{2,1,0:T(1,128)} async-done(((f32[32,1,16384]{2,1,0:T(1,128)}), f32[32,1,16384]{2,1,0:T(1,128)}, u32[]{:S(2)}, u32[]{:S(2)}) %all-to-all-start.1) | async-done | bytes 2097184 | tf_op jit(solution)/shard_map/all_to_all | solution.py:81
  267.5 7.4 %reduce.1 = f32[32,16384]{1,0:T(8,128)S(1)} reduce(f32[32,1,16384]{2,1,0:T(1,128)} %all-to-all-done.1, f32[]{:T(128)} %broadcast.102), dimensions={1}, to_apply=%all_to_all.25.reduce_sub_computation | reduce | bytes 4194308 | tf_op jit(solution)/shard_map/all_to_all | solution.py:81
  274.9 4.8 %reshape.107 = f32[1024,1,2,8,32]{4,3,2,1,0:T(8,128)} reshape(f32[32,16384]{1,0:T(8,128)S(1)} %reduce.1) | data formatting | bytes 4194304
  279.7 11.4 %copy.15 = f32[2,8,32,32,1,32]{5,3,2,1,0,4:T(8,128)} copy(f32[2,8,32,32,1,32]{5,1,0,2,3,4:T(8,128)} %bitcast.52) | data formatting | bytes 4194304 | tf_op jit(solution)/shard_map/all_to_all | solution.py:81
  291.1 6.9 %reshape.100 = f32[2,8,32,1024]{3,2,1,0:T(8,128)S(1)} reshape(f32[2,8,32,32,1,32]{5,3,2,1,0,4:T(8,128)} %copy.15) | data formatting | bytes 4194304 | tf_op jit(solution)/shard_map/reshape | solution.py:81
  298.0 2.7 multiply_reduce_fusion.1
  300.7 80.6 %all-reduce = (f32[]{:T(128)}, f32[]{:T(128)}) all-reduce(f32[]{:T(128)} %multiply_reduce_fusion.2, f32[]{:T(128)} %multiply_reduce_fusion.1), channel_id=1, replica_groups=mesh['chan'=32,'tm'=8] {'chan','tm'}, use_global_device_ids=true, to_apply=%region_1.2 | all-reduce | flops 2 | bytes 16 | tf_op jit(solution)/shard_map/psum | solution.py:57
  382.6 4.0 multiply_reduce_fusion
  386.7 73.0 %psum.23 = f32[]{:T(128)} all-reduce(f32[]{:T(128)} %get-tuple-element.5), channel_id=1, replica_groups=mesh['chan'=32,'tm'=8] {'chan','tm'}, use_global_device_ids=true, to_apply=%region_5.6 | all-reduce | flops 1 | bytes 8 | tf_op jit(solution)/shard_map/psum | solution.py:87
  461.0 6.0 %multiply_add_fusion = (f32[2,8,32,1024]{3,2,1,0:T(8,128)}, f32[2,8,32,1024]{3,2,1,0:T(8,128)}) fusion(f32[2,8,32,1024]{3,2,1,0:T(8,128)} %get-tuple-element.6, f32[2,8,32,1024]{3,2,1,0:T(8,128)} %param.6, f32[]{:T(128)S(6)} %div.78, f32[2,8,32,1024]{3,2,1,0:T(8,128)} %param.4, f32[]{:T(128)S(6)} %div.77), kind=kLoop, calls=%fused_computation.48 | loop fusion | flops 2097152 | bytes 10485768 | tf_op jit(solution)/shard_map/add | solution.py:89
  (19 shorter events, 7.8 us)
Async XLA Ops:
  24.4 60.4 %all-to-all-start = ((f32[32,1,16384]{2,1,0:T(1,128)}), f32[32,1,16384]{2,1,0:T(1,128)S(1)}, u32[]{:S(2)}, u32[]{:S(2)}) async-start(f32[32,1,16384]{2,1,0:T(1,128)} %reshape.104), calls=%async_computation | async-start | bytes 4194304 | tf_op jit(solution)/shard_map/all_to_all | solution.py:59
  84.8 1.3 copy-start.1
  120.9 37.8 %copy-start.3 = (f32[1,1,32,2048]{3,2,1,0:T(8,128)S(1)}, f32[1,1,32,2048]{3,2,1,0:T(8,128)}, u32[]{:S(2)}) copy-start(f32[1,1,32,2048]{3,2,1,0:T(8,128)} %param.7) | copy-start | bytes 786436
  139.8 8.6 %collective-permute-start = (f32[8,3,2048]{2,1,0:T(4,128)S(1)}, f32[8,3,2048]{2,1,0:T(4,128)S(1)}, u32[]{:S(2)}, u32[]{:S(2)}) collective-permute-start(f32[8,3,2048]{2,1,0:T(4,128)S(1)} %slice.66), channel_id=1, source_target_pairs={{248,0},{0,8},{8,16},{16,24},{24,32},{32,40},{40,48},{48,56},{56,6... | collective-permute-start | bytes 589832 | tf_op jit(solution)/shard_map/ppermute | solution.py:16
  148.5 10.2 %collective-permute-start.1 = (f32[8,3,2048]{2,1,0:T(4,128)S(1)}, f32[8,3,2048]{2,1,0:T(4,128)S(1)}, u32[]{:S(2)}, u32[]{:S(2)}) collective-permute-start(f32[8,3,2048]{2,1,0:T(4,128)S(1)} %collective-permute-done), channel_id=1, source_target_pairs={{0,1},{1,2},{2,3},{3,4},{4,5},{5,6},{6,7},{8,9},{9,10},{10,11},{11... | collective-permute-start | bytes 589832 | tf_op jit(solution)/shard_map/ppermute | solution.py:22
  159.8 1.3 copy-start.2
  161.2 5.3 %collective-permute-start.2 = (f32[8,3,2048]{2,1,0:T(4,128)S(1)}, f32[8,3,2048]{2,1,0:T(4,128)S(1)}, u32[]{:S(2)}, u32[]{:S(2)}) collective-permute-start(f32[8,3,2048]{2,1,0:T(4,128)S(1)} %slice.73), channel_id=1, source_target_pairs={{8,0},{16,8},{24,16},{32,24},{40,32},{48,40},{56,48},{64,56},{72,6... | collective-permute-start | bytes 589832 | tf_op jit(solution)/shard_map/ppermute | solution.py:16
  166.5 10.6 %collective-permute-start.3 = (f32[8,3,2048]{2,1,0:T(4,128)S(1)}, f32[8,3,2048]{2,1,0:T(4,128)S(1)}, u32[]{:S(2)}, u32[]{:S(2)}) collective-permute-start(f32[8,3,2048]{2,1,0:T(4,128)S(1)} %collective-permute-done.2), channel_id=1, source_target_pairs={{1,0},{2,1},{3,2},{4,3},{5,4},{6,5},{7,6},{9,8},{10,9},{11,10},{12... | collective-permute-start | bytes 589832 | tf_op jit(solution)/shard_map/ppermute | solution.py:22
  217.7 5.8 %copy-start = (f32[2,8,32,1024]{3,2,1,0:T(8,128)S(1)}, f32[2,8,32,1024]{3,2,1,0:T(8,128)}, u32[]{:S(2)}) copy-start(f32[2,8,32,1024]{3,2,1,0:T(8,128)} %param.5) | copy-start | bytes 6291460
  217.7 49.8 %all-to-all-start.1 = ((f32[32,1,16384]{2,1,0:T(1,128)}), f32[32,1,16384]{2,1,0:T(1,128)}, u32[]{:S(2)}, u32[]{:S(2)}) async-start(f32[32,1,16384]{2,1,0:T(1,128)} %reshape.106), calls=%async_computation.1 | async-start | bytes 4194304 | tf_op jit(solution)/shard_map/all_to_all | solution.py:81
where the time goes:
time: 476 us; the launch traced here: 467 us
  blocking collectives  154 us (32%)
  local copies, waits for them, and re-layouts  91 us (19%)
  waiting for transfers between devices  80.2 us (17%)
  other arithmetic  64.7 us (14%)
  matrix products  45.4 us (10%)
  starting transfers between devices  28.6 us (6%)
    psum x1, blocking collectives, per_device(): norm_now = lax.psum(jnp.sum(residual * residual), ('chan', 'tm'))  80.6 us
    psum x1, blocking collectives, per_device(): norm_next = lax.psum(jnp.sum(new_residual * new_residual), ('chan', 'tm'))  73 us
    all_to_all x1, waiting for transfers between devices, per_device(): lax.all_to_all(framed, 'chan', split_axis=2, concat_axis=3, tiled=True)  42.8 us
    neg x1, other arithmetic, dense_table(): return jnp.stack([jnp.cos(angle), -jnp.sin(angle)]) / math.sqrt(SAMPLES)  34.6 us
    unnamed x12, local copies, waits for them, and re-layouts  27.9 us
    dot_general x1, matrix products, to_spectra(): jnp.einsum('fmn,ckn->cfkm', weighted, tables, precision=lax.Precision.HIG...  26.6 us
    dot_general x1, matrix products, to_samples(): jnp.einsum('cfkm,ckn->fmn', spectra, tables, precision=lax.Precision.HIGH...  18.9 us
    reshape x2, local copies, waits for them, and re-layouts, per_device(): direction.reshape(lead, feeds_here, chans_here, group_count, block_len)  16 us
  transfers between devices with their start and end apart: 6, of which 6 were waited for; matrix products, arithmetic and copies ran while one was open for 8% of the time, Pallas kernels for 0%

commit v1 on v0

v1 whole, which is shorter than its diff:
```python
import math

import jax
import jax.numpy as jnp
import ml_dtypes
import numpy as np
from jax import lax
from jax.experimental import pallas as pl
from jax.experimental.pallas import tpu as pltpu
from jax.sharding import PartitionSpec as P

MESH = pl.DeviceIdType.MESH
F32 = jnp.float32
BF16 = jnp.bfloat16

SAMPLES = 2048
CHANNELS = 1024
TAPS = 4
FEEDS = 8
GROUPS = 32
SEGMENTS = 8
BLOCK = 32
KHERE = 32
HALF = 2
ACROSS = 4
LANES = ACROSS * BLOCK
RIM = 64
RADIX = 8
ROWS = SAMPLES // RADIX
QUARTER = 4
GQ = GROUPS // QUARTER
INNER = GQ * 2 * KHERE
ROOT_HALF = math.sqrt(0.5)


def tables():
    j = np.arange(CHANNELS // QUARTER)
    r = np.arange(ROWS)
    s = np.arange(RADIX)
    turns = (j[None, None, :] * (RADIX * r[None, :, None] + s[:, None, None])) % SAMPLES
    angle = 2.0 * np.pi * turns / SAMPLES
    scale = 1.0 / math.sqrt(SAMPLES)
    both = np.stack([np.cos(angle) * scale, -np.sin(angle) * scale], axis=2)
    both = both.reshape(RADIX, ROWS, 2, GQ, KHERE).transpose(0, 1, 3, 2, 4)
    full = both.reshape(RADIX, ROWS, INNER)
    high = full.astype(np.float32).astype(ml_dtypes.bfloat16)
    low = (full - high.astype(np.float64)).astype(np.float32).astype(ml_dtypes.bfloat16)
    forward = np.concatenate([high, low], axis=1)
    backward = np.concatenate([high.transpose(0, 2, 1), low.transpose(0, 2, 1)], axis=1)
    return forward, backward


def window_table():
    position = np.arange(TAPS * SAMPLES, dtype=np.float64)
    taper = 0.5 - 0.5 * np.cos(2.0 * np.pi * position / (TAPS * SAMPLES - 1))
    window = (np.sinc(position / SAMPLES - TAPS / 2) * taper).astype(np.float32)
    window = window.reshape(TAPS, ROWS, RADIX).transpose(0, 2, 1)
    return np.ascontiguousarray(np.broadcast_to(window[..., None], (TAPS, RADIX, ROWS, LANES)))


def copy_to(src, dst, ssem, rsem, device):
    return pltpu.make_async_remote_copy(
        src_ref=src, dst_ref=dst, send_sem=ssem, recv_sem=rsem, device_id=device, device_id_type=MESH
    )


def loop(n, body, init=None):
    if init is None:
        def plain(i, carry):
            body(i)
            return carry

        lax.fori_loop(0, n, plain, 0)
        return None
    return lax.fori_loop(0, n, body, init)


def fold_rows(x):
    rows, cols = x.shape
    total = None
    for i in range(rows // 8):
        for j in range(cols // LANES):
            y = x[8 * i : 8 * i + 8, LANES * j : LANES * (j + 1)]
            total = y if total is None else total + y
    return total


def exchange_kernel(
    sol_hbm, res_hbm, dir_hbm, wgt_hbm, tf_hbm, tb_hbm, win_hbm,
    nsol, nres, dirv, beta_ref,
    recvf, sendb, recvb, down_s, down_r, up_s, up_r,
    tf, tb, win, raw, nat, noise, bx, sm, st, bw, vv,
    part_c, part_t,
    load_sem, self_sem, fs, fr, bs, br, halo_s, halo_r, ns, nr, cs, cr, ts, tr,
):
    c = lax.axis_index("chan")
    t = lax.axis_index("tm")
    z, x_here = c // ACROSS, lax.rem(c, ACROSS)

    up_dev = (lax.rem(c + ACROSS, GROUPS), lax.rem(t + (c + ACROSS) // GROUPS, SEGMENTS))
    down_dev = (
        lax.rem(c + GROUPS - ACROSS, GROUPS),
        lax.rem(t + SEGMENTS - 1 + (c + GROUPS - ACROSS) // GROUPS, SEGMENTS),
    )
    barrier = pltpu.get_barrier_semaphore()

    def greet_chan(i):
        pl.semaphore_signal(
            barrier, inc=1, device_id=(lax.rem(c + i + 1, GROUPS), t), device_id_type=MESH
        )

    def greet_tm(i):
        pl.semaphore_signal(
            barrier, inc=1, device_id=(c, lax.rem(t + i + 1, SEGMENTS)), device_id_type=MESH
        )

    loads = [
        pltpu.make_async_copy(src, dst, load_sem.at[i])
        for i, (src, dst) in enumerate(
            (
                (dir_hbm, dirv),
                (wgt_hbm.at[0, 0], raw.at[x_here]),
                (res_hbm, nres),
                (tf_hbm, tf),
                (win_hbm, win),
                (tb_hbm, tb),
                (sol_hbm, nsol),
            )
        )
    ]
    for cp in loads:
        cp.start()
    loop(GROUPS - 1, greet_chan)
    loop(SEGMENTS - 1, greet_tm)
    pl.semaphore_signal(barrier, inc=1, device_id=up_dev, device_id_type=MESH)
    pl.semaphore_signal(barrier, inc=1, device_id=down_dev, device_id_type=MESH)

    def frames_of(zz):
        return pl.ds(pl.multiple_of(zz * LANES, LANES), LANES)

    def forward_copy(h, i):
        d = lax.rem(c + i + 1, GROUPS)
        src = dirv.at[:, HALF * lax.rem(d, ACROSS) + h, :, frames_of(d // ACROSS)]
        return copy_to(src, recvf.at[h, c], fs.at[h, d], fr.at[h, c], (d, t))

    def forward_arrival(h, i):
        d = lax.rem(c + GROUPS - 1 - i, GROUPS)
        return copy_to(recvf.at[h, d], recvf.at[h, d], fs.at[h, d], fr.at[h, d], (d, t))

    def backward_copy(h, i):
        d = lax.rem(c + i + 1, GROUPS)
        dst = recvb.at[:, HALF * x_here + h, :, frames_of(z)]
        return copy_to(sendb.at[h, d], dst, bs.at[h, d], br.at[h, c], (d, t))

    def backward_arrival(h, i):
        d = lax.rem(c + GROUPS - 1 - i, GROUPS)
        dst = recvb.at[:, HALF * lax.rem(d, ACROSS) + h, :, frames_of(d // ACROSS)]
        return copy_to(sendb.at[h, d], dst, bs.at[h, d], br.at[h, d], (d, t))

    def noise_copy(i):
        xx = lax.rem(x_here + i + 1, ACROSS)
        return copy_to(
            raw.at[x_here], raw.at[x_here], ns.at[xx], nr.at[x_here], (z * ACROSS + xx, t)
        )

    def noise_arrival(i):
        xx = lax.rem(x_here + i + 1, ACROSS)
        return copy_to(raw.at[xx], raw.at[xx], ns.at[xx], nr.at[xx], (z * ACROSS + xx, t))

    here = (HALF * x_here, frames_of(z))
    self_f = [
        pltpu.make_async_copy(dirv.at[:, here[0] + h, :, here[1]], recvf.at[h, c], self_sem.at[0, h])
        for h in range(HALF)
    ]
    self_b = [
        pltpu.make_async_copy(sendb.at[h, c], recvb.at[:, here[0] + h, :, here[1]], self_sem.at[1, h])
        for h in range(HALF)
    ]

    loads[0].wait()
    for h in range(HALF):
        self_f[h].start()
    pl.semaphore_wait(barrier, GROUPS - 1 + SEGMENTS - 1 + 2)
    loop(GROUPS - 1, lambda i: forward_copy(0, i).start())
    loads[1].wait()
    loop(ACROSS - 1, lambda i: noise_copy(i).start())
    loop(GROUPS - 1, lambda i: forward_copy(1, i).start())

    loads[2].wait()

    def square(i, acc):
        part, f = i // FEEDS, lax.rem(i, FEEDS)
        y = nres[part, f]
        return acc + fold_rows(y * y)

    norm_part = loop(2 * FEEDS, square, jnp.zeros((8, LANES), F32))

    loop(ACROSS - 1, lambda i: noise_arrival(i).wait_recv())

    def turn(i):
        cols = pl.ds(pl.multiple_of(i * 128, 128), 128)
        nat[cols, :] = jnp.concatenate([raw[q, :, cols] for q in range(ACROSS)], axis=0).T

    loop(SAMPLES // 128, turn)
    for s in range(RADIX):
        noise[s] = nat[pl.ds(s, ROWS, stride=RADIX), :]
    for cp in loads[3:]:
        cp.wait()

    keep_down = jnp.where((z == 0) & (t == 0), 0.0, 1.0).astype(F32)
    keep_up = jnp.where((z == GROUPS // ACROSS - 1) & (t == SEGMENTS - 1), 0.0, 1.0).astype(F32)

    def split_store(ref, where, x):
        high = x.astype(BF16)
        low = (x - high.astype(F32)).astype(BF16)
        ref[where + (slice(0, LANES),)] = high
        ref[where + (slice(LANES, 2 * LANES),)] = low

    def quadrants(x, rows):
        return (x[:rows, :LANES] + x[:rows, LANES:]) + (x[rows:, :LANES] + x[rows:, LANES:])

    RB = 16
    lane = lax.broadcasted_iota(jnp.int32, (RB, LANES), 1)
    slot = lane // TAPS
    GROUP_ROWS = [(s, q) for s in range(RADIX) for q in range(ROWS // RIM)]

    def rolled(x, by):
        by = by % LANES
        return pltpu.roll(x, by, 1) if by else x

    def fold_in(h):
        def body(g):
            re = [recvf[h, p * GQ + g, 0] for p in range(QUARTER)]
            im = [recvf[h, p * GQ + g, 1] for p in range(QUARTER)]

            def pairs(a, b):
                return [
                    (re[a] + re[b], im[a] + im[b]),
                    (re[a] - im[b], im[a] + re[b]),
                    (re[a] - re[b], im[a] - im[b]),
                    (re[a] + im[b], im[a] - re[b]),
                ]

            u, v = pairs(0, 2), pairs(1, 3)
            w = [
                v[0],
                ((v[1][0] - v[1][1]) * ROOT_HALF, (v[1][0] + v[1][1]) * ROOT_HALF),
                (-v[2][1], v[2][0]),
                (-(v[3][0] + v[3][1]) * ROOT_HALF, (v[3][0] - v[3][1]) * ROOT_HALF),
            ]
            for s in range(4):
                for part in range(2):
                    split_store(bx, (s, g, part, slice(None)), u[s][part] + w[s][part])
                    split_store(bx, (s + 4, g, part, slice(None)), u[s][part] - w[s][part])

        loop(GQ, body)

    def to_samples():
        def body(s):
            x = bx[s].reshape(INNER, 2 * LANES)
            sm[s] = quadrants(jnp.dot(tf[s], x, preferred_element_type=F32), ROWS)

        loop(RADIX, body)

    def pack_down(h):
        def body(i):
            out = jnp.zeros((RB, LANES), F32)
            for n, (s, q) in enumerate(GROUP_ROWS):
                rows = pl.ds(pl.multiple_of(q * RIM + i * RB, RB), RB)
                out = jnp.where(slot == n, rolled(sm[s, rows, :], TAPS * n + TAPS), out)
            down_s[h, pl.ds(pl.multiple_of(i * RB, RB), RB), :] = out

        loop(RIM // RB, body)

    def make_stream(h, acc):
        def body(i, acc):
            packed = pl.ds(pl.multiple_of(i * RB, RB), RB)
            below = down_r[h, packed, :] * keep_down
            out = jnp.zeros((RB, LANES), F32)
            for n, (s, q) in enumerate(GROUP_ROWS):
                rows = pl.ds(pl.multiple_of(q * RIM + i * RB, RB), RB)
                x = sm[s, rows, :]
                rim = rolled(below, -TAPS * n - TAPS)
                total = win[0, s, rows, :] * x
                for k in range(1, TAPS):
                    total = total + win[k, s, rows, :] * rolled(jnp.where(lane >= LANES - k, rim, x), k)
                y = noise[s, rows, :] * total
                st[s, rows, :] = y
                acc = acc + fold_rows(y * total)
                out = jnp.where(slot == n, rolled(y, TAPS * n), out)
            up_s[h, packed, :] = out
            return acc

        return loop(RIM // RB, body, acc)

    def make_weighted(h):
        def body(i):
            packed = pl.ds(pl.multiple_of(i * RB, RB), RB)
            above = up_r[h, packed, :] * keep_up
            for n, (s, q) in enumerate(GROUP_ROWS):
                rows = pl.ds(pl.multiple_of(q * RIM + i * RB, RB), RB)
                x = st[s, rows, :]
                rim = rolled(above, -TAPS * n)
                total = win[0, s, rows, :] * x
                for k in range(1, TAPS):
                    total = total + win[k, s, rows, :] * rolled(jnp.where(lane < k, rim, x), -k)
                split_store(bw, (s, rows), total)

        loop(RIM // RB, body)

    def to_spectra():
        def body(s):
            x = quadrants(jnp.dot(tb[s], bw[s], preferred_element_type=F32), INNER)
            vv[s] = x.reshape(GQ, 2, KHERE, LANES)

        loop(RADIX, body)

    def fold_out(h):
        def body(g):
            re = [vv[s, g, 0] for s in range(RADIX)]
            im = [vv[s, g, 1] for s in range(RADIX)]
            ar = [re[s] + re[s + 4] for s in range(4)]
            ai = [im[s] + im[s + 4] for s in range(4)]
            dr = [re[s] - re[s + 4] for s in range(4)]
            di = [im[s] - im[s + 4] for s in range(4)]
            one = ((dr[1] + di[1]) * ROOT_HALF, (di[1] - dr[1]) * ROOT_HALF)
            one3 = ((di[1] - dr[1]) * ROOT_HALF, -(di[1] + dr[1]) * ROOT_HALF)
            three = ((di[3] - dr[3]) * ROOT_HALF, -(di[3] + dr[3]) * ROOT_HALF)
            three3 = ((dr[3] + di[3]) * ROOT_HALF, (di[3] - dr[3]) * ROOT_HALF)
            image = [
                ((ar[0] + ar[2]) + (ar[1] + ar[3]), (ai[0] + ai[2]) + (ai[1] + ai[3])),
                ((dr[0] + di[2]) + (one[0] + three[0]), (di[0] - dr[2]) + (one[1] + three[1])),
                ((ar[0] - ar[2]) + (ai[1] - ai[3]), (ai[0] - ai[2]) + (ar[3] - ar[1])),
                ((dr[0] - di[2]) + (one3[0] + three3[0]), (di[0] + dr[2]) + (one3[1] + three3[1])),
            ]
            for p in range(QUARTER):
                for part in range(2):
                    sendb[h, p * GQ + g, part] = image[p][part]

        loop(GQ, body)

    def tm_copy(rnd, i):
        d = lax.rem(t + i + 1, SEGMENTS)
        return copy_to(part_t.at[rnd, t], part_t.at[rnd, t], ts.at[rnd, d], tr.at[rnd, t], (c, d))

    def tm_arrival(rnd, i):
        d = lax.rem(t + i + 1, SEGMENTS)
        return copy_to(part_t.at[rnd, d], part_t.at[rnd, d], ts.at[rnd, d], tr.at[rnd, d], (c, d))

    def chan_copy(rnd, i):
        d = lax.rem(c + i + 1, GROUPS)
        return copy_to(part_c.at[rnd, c], part_c.at[rnd, c], cs.at[rnd, d], cr.at[rnd, c], (d, t))

    def chan_arrival(rnd, i):
        d = lax.rem(c + i + 1, GROUPS)
        return copy_to(part_c.at[rnd, d], part_c.at[rnd, d], cs.at[rnd, d], cr.at[rnd, d], (d, t))

    def sum_start(rnd, row):
        part_t[rnd, t] = row
        loop(SEGMENTS - 1, lambda i: tm_copy(rnd, i).start())

    def sum_middle(rnd):
        loop(SEGMENTS - 1, lambda i: tm_arrival(rnd, i).wait_recv())
        part_c[rnd, c] = jnp.sum(part_t[rnd], axis=0)
        loop(GROUPS - 1, lambda i: chan_copy(rnd, i).start())

    def sum_end(rnd):
        loop(GROUPS - 1, lambda i: chan_arrival(rnd, i).wait_recv())
        total = jnp.sum(part_c[rnd], axis=0)
        loop(SEGMENTS - 1, lambda i: tm_copy(rnd, i).wait_send())
        loop(GROUPS - 1, lambda i: chan_copy(rnd, i).wait_send())
        return total

    lane_row = lax.broadcasted_iota(jnp.int32, (1, LANES), 1)

    def both(first, second):
        a = jnp.sum(first, axis=0, keepdims=True)
        b = jnp.sum(second, axis=0, keepdims=True)
        half = LANES // 2
        return jnp.where(lane_row < half, a + pltpu.roll(a, half, 1), b + pltpu.roll(b, half, 1))

    curve = jnp.zeros((8, LANES), F32)
    for h in range(HALF):
        self_f[h].wait()
        loop(GROUPS - 1, lambda i: forward_arrival(h, i).wait_recv())
        fold_in(h)
        to_samples()
        pack_down(h)
        down = copy_to(down_s.at[h], down_r.at[h], halo_s.at[0, h], halo_r.at[0, h], up_dev)
        down.start()
        down.wait_recv()
        curve = make_stream(h, curve)
        up = copy_to(up_s.at[h], up_r.at[h], halo_s.at[1, h], halo_r.at[1, h], down_dev)
        up.start()
        if h == HALF - 1:
            sum_start(0, both(norm_part, curve))
        up.wait_recv()
        make_weighted(h)
        to_spectra()
        fold_out(h)
        if h == HALF - 1:
            sum_middle(0)
        loop(GROUPS - 1, lambda i: backward_copy(h, i).start())
        self_b[h].start()
        down.wait_send()
        up.wait_send()

    sums = sum_end(0)
    zero = jnp.zeros((1, LANES), F32)
    norm_now = jnp.sum(jnp.where(lane_row < LANES // 2, sums, zero), axis=1, keepdims=True)
    alpha = norm_now / jnp.sum(jnp.where(lane_row < LANES // 2, zero, sums), axis=1, keepdims=True)

    def step_solution(i):
        part, f = i // FEEDS, lax.rem(i, FEEDS)
        nsol[part, f] = nsol[part, f] + alpha * dirv[part, f]

    loop(2 * FEEDS, step_solution)

    norm_next = jnp.zeros((8, LANES), F32)
    for h in range(HALF):
        self_b[h].wait()
        loop(GROUPS - 1, lambda i: backward_arrival(h, i).wait_recv())

        def update(i, acc):
            part, f = i // ACROSS, HALF * lax.rem(i, ACROSS) + h
            y = nres[part, f] - alpha * recvb[part, f]
            nres[part, f] = y
            return acc + fold_rows(y * y)

        norm_next = loop(2 * ACROSS, update, norm_next)

    sum_start(1, jnp.sum(norm_next, axis=0, keepdims=True))
    sum_middle(1)
    total = jnp.sum(sum_end(1), axis=1, keepdims=True)
    beta_ref[...] = jnp.broadcast_to(total / norm_now, (8, LANES))
    for h in range(HALF):
        loop(GROUPS - 1, lambda i: forward_copy(h, i).wait_send())
        loop(GROUPS - 1, lambda i: backward_copy(h, i).wait_send())
    loop(ACROSS - 1, lambda i: noise_copy(i).wait_send())


def finish_kernel(nsol, nres, dirv, beta_ref, sol_out, res_out, dir_out, ndir, sem):
    copies = [
        pltpu.make_async_copy(nsol, sol_out, sem.at[0]),
        pltpu.make_async_copy(nres, res_out, sem.at[1]),
    ]
    for cp in copies:
        cp.start()
    beta = beta_ref[0:1, 0:1]
    for part in range(2):
        def body(f):
            ndir[part, f] = nres[part, f] + beta * dirv[part, f]

        loop(FEEDS, body)
        cp = pltpu.make_async_copy(ndir.at[part], dir_out.at[part], sem.at[2 + part])
        cp.start()
        copies.append(cp)
    for cp in copies:
        cp.wait()


def per_device(solution_, residual, direction, sample_weight):
    forward, backward = tables()
    window = window_table()
    shape = direction.shape
    vmem = pl.BlockSpec(memory_space=pltpu.VMEM)
    hbm = pl.BlockSpec(memory_space=pl.ANY)
    dma = pltpu.SemaphoreType.DMA
    piece = (2, KHERE, LANES)
    nsol, nres, dirv, beta = pl.pallas_call(
        exchange_kernel,
        name="exchange",
        out_shape=[pltpu.VMEM(shape, F32)] * 3 + [pltpu.VMEM((8, LANES), F32)],
        in_specs=[hbm] * 7,
        out_specs=[vmem] * 4,
        scratch_shapes=[
            pltpu.VMEM((HALF, GROUPS) + piece, F32),
            pltpu.VMEM((HALF, GROUPS) + piece, F32),
            pltpu.VMEM(shape, F32),
            pltpu.VMEM((HALF, RIM, LANES), F32),
            pltpu.VMEM((HALF, RIM, LANES), F32),
            pltpu.VMEM((HALF, RIM, LANES), F32),
            pltpu.VMEM((HALF, RIM, LANES), F32),
            pltpu.VMEM(forward.shape, BF16),
            pltpu.VMEM(backward.shape, BF16),
            pltpu.VMEM(window.shape, F32),
            pltpu.VMEM((ACROSS, BLOCK, SAMPLES), F32),
            pltpu.VMEM((SAMPLES, LANES), F32),
            pltpu.VMEM((RADIX, ROWS, LANES), F32),
            pltpu.VMEM((RADIX, GQ, 2, KHERE, 2 * LANES), BF16),
            pltpu.VMEM((RADIX, ROWS, LANES), F32),
            pltpu.VMEM((RADIX, ROWS, LANES), F32),
            pltpu.VMEM((RADIX, ROWS, 2 * LANES), BF16),
            pltpu.VMEM((RADIX, GQ, 2, KHERE, LANES), F32),
            pltpu.VMEM((2, GROUPS, 1, LANES), F32),
            pltpu.VMEM((2, SEGMENTS, 1, LANES), F32),
            dma((7,)),
            dma((2, HALF)),
            dma((HALF, GROUPS)),
            dma((HALF, GROUPS)),
            dma((HALF, GROUPS)),
            dma((HALF, GROUPS)),
            dma((2, HALF)),
            dma((2, HALF)),
            dma((ACROSS,)),
            dma((ACROSS,)),
            dma((2, GROUPS)),
            dma((2, GROUPS)),
            dma((2, SEGMENTS)),
            dma((2, SEGMENTS)),
        ],
        compiler_params=pltpu.CompilerParams(
            collective_id=0, has_side_effects=True, vmem_limit_bytes=52 * 2**20
        ),
    )(solution_, residual, direction, sample_weight, forward, backward, window)
    inside = [pltpu.with_memory_space_constraint(x, pltpu.VMEM) for x in (nsol, nres, dirv, beta)]
    return pl.pallas_call(
        finish_kernel,
        name="finish",
        out_shape=[jax.ShapeDtypeStruct(shape, F32)] * 3,
        in_specs=[vmem] * 4,
        out_specs=[hbm] * 3,
        scratch_shapes=[pltpu.VMEM(shape, F32), dma((4,))],
        compiler_params=pltpu.CompilerParams(vmem_limit_bytes=24 * 2**20),
    )(*inside)


def solution(mesh):
    placed = P(None, None, "chan", "tm")
    return jax.shard_map(
        per_device,
        mesh=mesh,
        in_specs=(placed, placed, placed, P("tm", "chan", None, None)),
        out_specs=(placed, placed, placed),
        check_vma=False,
    )
```

time: 476 us -> 160 us (0.34); the launches traced: 467 us -> 160 us
  Pallas kernels: 0 us -> 159 us
  blocking collectives: 154 us -> 0 us
  local copies, waits for them, and re-layouts: 91 us -> 0 us
  waiting for transfers between devices: 80.2 us -> 0 us
  other arithmetic: 64.7 us -> 0 us
  matrix products: 45.4 us -> 0 us
  starting transfers between devices: 28.6 us -> 0 us
    pallas_call x0 -> x2, Pallas kernels: none -> 159 us  [the longest x1 156 us: per_device(): pl.pallas_call(exchange_kernel, name='exchange', out_shape=[pltpu.VMEM(sh...]
    psum x2 -> x0, blocking collectives: 154 us -> none  [the longest x1 80.6 us: per_device(): norm_now = lax.psum(jnp.sum(residual * residual), ('chan', 'tm'))]
    all_to_all x2 -> x0, waiting for transfers between devices: 56.7 us -> none  [the longest x1 42.8 us: per_device(): lax.all_to_all(framed, 'chan', split_axis=2, concat_axis=3, tiled=True)]
    dot_general x2 -> x0, matrix products: 45.4 us -> none  [the longest x1 26.6 us: to_spectra(): jnp.einsum('fmn,ckn->cfkm', weighted, tables, precision=lax.Precision.HIG...]
    neg x1 -> x0, other arithmetic: 34.6 us -> none  [dense_table(): return jnp.stack([jnp.cos(angle), -jnp.sin(angle)]) / math.sqrt(SAMPLES)]
    unnamed x12 -> x0, local copies, waits for them, and re-layouts: 27.9 us -> none
    all_to_all x4 -> x0, local copies, waits for them, and re-layouts: 26.1 us -> none  [the longest x3 14.7 us: per_device(): lax.all_to_all(sectioned, 'chan', split_axis=3, concat_axis=2, tiled=True)]
    ppermute x4 -> x0, waiting for transfers between devices: 23.5 us -> none  [the longest x2 12 us: passed_along(): return lax.ppermute(block, axis, route)]
  transfers between devices with their start and end apart: 6 -> 0, of which waited for: 6 -> 0; matrix products, arithmetic and copies ran while one was open for 8% -> 0% of each run, Pallas kernels for 0% -> 0%
where the time goes in v1:
time: 160 us
  Pallas kernels  159 us (99%)
    pallas_call x1, Pallas kernels, per_device(): pl.pallas_call(exchange_kernel, name='exchange', out_shape=[pltpu.VMEM(sh...  156 us

profile of v1, /device:TPU:1, one launch (start us, length us, event | category | flops | bytes accessed | tf_op | source)
XLA Modules:
  0.0 159.7 jit_solution(6720723952735730682)
XLA Ops:
  0.6 156.4 %exchange.1 = (f32[2,8,32,1024]{3,2,1,0:T(8,128)S(1)}, f32[2,8,32,1024]{3,2,1,0:T(8,128)S(1)}, f32[2,8,32,1024]{3,2,1,0:T(8,128)S(1)}, f32[8,128]{1,0:T(8,128)S(1)}) custom-call(f32[2,8,32,1024]{3,2,1,0:T(8,128)} %sol_hbm.1, f32[2,8,32,1024]{3,2,1,0:T(8,128)} %res_hbm.1, f32[2,8,32,1024]{3,2,1,0:T(8,128)} %dir_hbm.1, f32[1,1,32,2048]{3,2,1,0:T(8,128)} %wgt_hbm.1, ...), custom_call_target="tpu_custom_call" | custom-call | tf_op jit(solution)/shard_map/exchange/pallas_call | solution.py:470
  157.0 2.7 %finish.1 = (f32[2,8,32,1024]{3,2,1,0:T(8,128)}, f32[2,8,32,1024]{3,2,1,0:T(8,128)}, f32[2,8,32,1024]{3,2,1,0:T(8,128)}) custom-call(f32[2,8,32,1024]{3,2,1,0:T(8,128)S(1)} %get-tuple-element.7.nsol, f32[2,8,32,1024]{3,2,1,0:T(8,128)S(1)} %get-tuple-element.8.nres, f32[2,8,32,1024]{3,2,1,0:T(8,128)S(1)} %get-tuple-element.9.dirv, ...), custom_call_target="tpu_custom_call" | custom-call | tf_op jit(solution)/shard_map/finish/pallas_call | solution.py:517

commit v2 on v1

v2 whole, which is shorter than its diff:
```python
import math

import jax
import jax.numpy as jnp
import ml_dtypes
import numpy as np
from jax import lax
from jax.experimental import pallas as pl
from jax.experimental.pallas import tpu as pltpu
from jax.sharding import PartitionSpec as P

MESH = pl.DeviceIdType.MESH
F32 = jnp.float32
BF16 = jnp.bfloat16

SAMPLES = 2048
CHANNELS = 1024
TAPS = 4
FEEDS = 8
GROUPS = 32
SEGMENTS = 8
BLOCK = 32
KHERE = 32
HALF = 2
ACROSS = 4
LANES = ACROSS * BLOCK
TILES = SAMPLES // LANES
RIM = 16
MAIN = 2 * LANES
STACK = MAIN + 2 * RIM
RADIX = 8
ROWS = SAMPLES // RADIX
QUARTER = 4
GQ = GROUPS // QUARTER
INNER = GQ * 2 * KHERE
ROOT_HALF = math.sqrt(0.5)
PEERS = GROUPS - 1
ROWS_Z = GROUPS // ACROSS


def tables():
    j = np.arange(CHANNELS // QUARTER)
    r = np.arange(ROWS)
    s = np.arange(RADIX)
    turns = (j[None, None, :] * (RADIX * r[None, :, None] + s[:, None, None])) % SAMPLES
    angle = 2.0 * np.pi * turns / SAMPLES
    scale = 1.0 / math.sqrt(SAMPLES)
    both = np.stack([np.cos(angle) * scale, -np.sin(angle) * scale], axis=1)
    full = both.transpose(0, 1, 3, 2).reshape(RADIX, INNER, ROWS)
    high = full.astype(np.float32).astype(ml_dtypes.bfloat16)
    low = (full - high.astype(np.float64)).astype(np.float32).astype(ml_dtypes.bfloat16)
    forward = np.concatenate([high, low], axis=2)
    backward = np.concatenate([high.transpose(0, 2, 1), low.transpose(0, 2, 1)], axis=2)
    return forward, backward


def window_table():
    position = np.arange(TAPS * SAMPLES, dtype=np.float64)
    taper = 0.5 - 0.5 * np.cos(2.0 * np.pi * position / (TAPS * SAMPLES - 1))
    window = (np.sinc(position / SAMPLES - TAPS / 2) * taper).astype(np.float32)
    window = window.reshape(TAPS, ROWS, RADIX).transpose(0, 2, 1).reshape(TAPS, TILES, 1, LANES)
    return np.ascontiguousarray(np.broadcast_to(window, (TAPS, TILES, 8, LANES)))


def copy_to(src, dst, ssem, rsem, device):
    return pltpu.make_async_remote_copy(
        src_ref=src, dst_ref=dst, send_sem=ssem, recv_sem=rsem, device_id=device, device_id_type=MESH
    )


def loop(n, body, init=None):
    if init is None:
        def plain(i, carry):
            body(i)
            return carry

        lax.fori_loop(0, n, plain, 0)
        return None
    return lax.fori_loop(0, n, body, init)


def fold_rows(x):
    rows, cols = x.shape
    total = None
    for i in range(rows // 8):
        for j in range(cols // LANES):
            y = x[8 * i : 8 * i + 8, LANES * j : LANES * (j + 1)]
            total = y if total is None else total + y
    return total


def exchange_kernel(
    sol_hbm, res_hbm, dir_hbm, wgt_hbm, tf_hbm, tb_hbm, win_hbm,
    nsol, nres, dirv, beta_ref,
    recvf, sendb, recvb, rim_s, rim_r, back_s, back_r, rim_v,
    tf, tb, win, raw, nat, noise, xt, bx, sm, st, bw, vv,
    part_c, part_t,
    load_sem, self_sem, fs, fr, bs, br, rim_sent, rim_got, ns, nr, cs, cr, ts, tr,
):
    c = lax.axis_index("chan")
    t = lax.axis_index("tm")
    z, x_here = c // ACROSS, lax.rem(c, ACROSS)

    some_dev = (lax.rem(c + 1, GROUPS), t)
    t_up = lax.rem(t + 1, SEGMENTS)
    t_down = lax.rem(t + SEGMENTS - 1, SEGMENTS)
    barrier = pltpu.get_barrier_semaphore()

    def greet_chan(i):
        pl.semaphore_signal(
            barrier, inc=1, device_id=(lax.rem(c + i + 1, GROUPS), t), device_id_type=MESH
        )

    def greet_tm(i):
        pl.semaphore_signal(
            barrier, inc=1, device_id=(c, lax.rem(t + i + 1, SEGMENTS)), device_id_type=MESH
        )

    loads = [
        pltpu.make_async_copy(src, dst, load_sem.at[i])
        for i, (src, dst) in enumerate(
            (
                (dir_hbm, dirv),
                (wgt_hbm.at[0, 0], raw.at[x_here]),
                (res_hbm, nres),
                (tf_hbm, tf),
                (win_hbm, win),
                (tb_hbm, tb),
                (sol_hbm, nsol),
            )
        )
    ]
    for cp in loads:
        cp.start()
    loop(GROUPS - 1, greet_chan)
    loop(SEGMENTS - 1, greet_tm)

    def greet_up(i):
        pl.semaphore_signal(barrier, inc=1, device_id=(i, t_up), device_id_type=MESH)

    def greet_down(i):
        pl.semaphore_signal(barrier, inc=1, device_id=(i, t_down), device_id_type=MESH)

    loop(ACROSS, greet_up)

    @pl.when(z == 0)
    def _():
        loop(GROUPS, greet_down)

    def frames_of(zz):
        return pl.ds(pl.multiple_of(zz * LANES, LANES), LANES)

    def forward_copy(h, i):
        d = lax.rem(c + i + 1, GROUPS)
        src = dirv.at[:, HALF * lax.rem(d, ACROSS) + h, :, frames_of(d // ACROSS)]
        return copy_to(src, recvf.at[h, c], fs.at[h], fr.at[h], (d, t))

    def forward_all(h):
        some = recvf.at[h, pl.ds(0, GROUPS - 1)]
        return copy_to(some, some, fs.at[h], fr.at[h], some_dev)

    def backward_copy(h, i):
        d = lax.rem(c + i + 1, GROUPS)
        dst = recvb.at[:, HALF * x_here + h, :, frames_of(z)]
        return copy_to(sendb.at[h, d], dst, bs.at[h], br.at[h], (d, t))

    def backward_all(h):
        some = sendb.at[h, pl.ds(0, GROUPS - 1)]
        return copy_to(some, some, bs.at[h], br.at[h], some_dev)

    def noise_copy(i):
        xx = lax.rem(x_here + i + 1, ACROSS)
        return copy_to(raw.at[x_here], raw.at[x_here], ns.at[0], nr.at[0], (z * ACROSS + xx, t))

    def noise_all():
        some = raw.at[pl.ds(0, ACROSS - 1)]
        return copy_to(some, some, ns.at[0], nr.at[0], some_dev)

    def rim_to(n):
        zz, xx = n // ACROSS, lax.rem(n, ACROSS)
        cc = lax.rem((zz + 1) * ACROSS + xx, GROUPS)
        tt = jnp.where(zz == ROWS_Z - 1, t_up, t)
        src = rim_s.at[zz, xx // 2]
        remote = copy_to(src, rim_r.at[c], rim_sent.at[0], rim_got.at[0], (cc, tt))
        return (zz + 1) * ACROSS + xx == c, remote, pltpu.make_async_copy(src, rim_r.at[c], self_sem.at[2, 0])

    def rim_back(n):
        tt = jnp.where(z == 0, t_down, t)
        remote = copy_to(back_s.at[n], back_r.at[c], rim_sent.at[1], rim_got.at[1], (n, tt))
        own = (n == c) & (z > 0)
        return own, remote, pltpu.make_async_copy(back_s.at[n], back_r.at[c], self_sem.at[2, 1])

    def rim_start(which):
        def body(n):
            own, remote, local = which(n)

            @pl.when(own)
            def _():
                local.start()

            @pl.when(jnp.logical_not(own))
            def _():
                remote.start()

        loop(GROUPS, body)

    def rim_wait(k, sent):
        buf = rim_r if k == 0 else back_r

        def whole(n):
            some = buf.at[pl.ds(0, n)]
            cp = copy_to(some, some, rim_sent.at[k], rim_got.at[k], some_dev)
            if sent:
                cp.wait_send()
            else:
                cp.wait_recv()

        @pl.when(z == 0)
        def _():
            whole(GROUPS)

        @pl.when(z > 0)
        def _():
            whole(PEERS)
            if not sent:
                pltpu.make_async_copy(buf.at[c], buf.at[c], self_sem.at[2, k]).wait()

    here = (HALF * x_here, frames_of(z))
    self_f = [
        pltpu.make_async_copy(dirv.at[:, here[0] + h, :, here[1]], recvf.at[h, c], self_sem.at[0, h])
        for h in range(HALF)
    ]
    self_b = [
        pltpu.make_async_copy(sendb.at[h, c], recvb.at[:, here[0] + h, :, here[1]], self_sem.at[1, h])
        for h in range(HALF)
    ]

    loads[0].wait()
    for h in range(HALF):
        self_f[h].start()
    pl.semaphore_wait(barrier, PEERS + SEGMENTS - 1 + ACROSS + jnp.where(z == 0, GROUPS, 0))
    loop(GROUPS - 1, lambda i: forward_copy(0, i).start())

    def pack_rim(n):
        zz, fh = n // 2, lax.rem(n, 2)
        for part in range(2):
            y = jnp.concatenate([dirv[part, 4 * fh + f, :, frames_of(zz)] for f in range(4)], axis=0).T
            rim_s[zz, fh, TAPS * part : TAPS * (part + 1), :] = y[LANES - TAPS :, :]

    loop(2 * ROWS_Z, pack_rim)
    rim_start(rim_to)
    loads[1].wait()
    loop(ACROSS - 1, lambda i: noise_copy(i).start())
    loop(GROUPS - 1, lambda i: forward_copy(1, i).start())

    loads[2].wait()

    def square(i, acc):
        part, f = i // FEEDS, lax.rem(i, FEEDS)
        y = nres[part, f]
        return acc + fold_rows(y * y)

    norm_part = loop(2 * FEEDS, square, jnp.zeros((8, LANES), F32))

    noise_all().wait_recv()

    def turn(i):
        cols = pl.ds(pl.multiple_of(i * 128, 128), 128)
        nat[cols, :] = jnp.concatenate([raw[q, :, cols] for q in range(ACROSS)], axis=0).T

    loop(SAMPLES // 128, turn)
    for n in range(TILES):
        first = n // 2 + (n % 2) * (SAMPLES // 2)
        noise[n] = nat[pl.ds(first, LANES, stride=RADIX), :].T
    for cp in loads[3:]:
        cp.wait()

    keep_down = jnp.where((z == 0) & (t == 0), 0.0, 1.0).astype(F32)
    blank = jnp.zeros((8, LANES), F32)
    for n in range(TILES):
        st[n, 0:8, :] = blank
        st[n, 8 + LANES : 16 + LANES, :] = blank

    def split(x):
        high = x.astype(BF16)
        return high, (x - high.astype(F32)).astype(BF16)

    def quadrants(x):
        cols = x.shape[1] // 2

        def joined(a, b, n):
            return (x[a : a + n, :cols] + x[a : a + n, cols:]) + (x[b : b + n, :cols] + x[b : b + n, cols:])

        return joined(0, LANES, LANES), joined(MAIN, MAIN + RIM, 8)

    def rim_store(ref, s, cols, x):
        high, low = split(jnp.concatenate([x, jnp.zeros((RIM - 8, LANES), F32)], axis=0))
        ref[s, MAIN : MAIN + RIM, cols] = high
        ref[s, MAIN + RIM : STACK, cols] = low

    lane8 = lax.broadcasted_iota(jnp.int32, (8, LANES), 1)
    odd_x = jnp.full((8, LANES), lax.rem(x_here, 2), jnp.int32) == 1

    def rolled(x, by):
        by = by % LANES
        return pltpu.roll(x, by, 1) if by else x

    RB = 16

    def turned(re, im):
        def pairs(a, b):
            return [
                (re[a] + re[b], im[a] + im[b]),
                (re[a] - im[b], im[a] + re[b]),
                (re[a] - re[b], im[a] - im[b]),
                (re[a] + im[b], im[a] - re[b]),
            ]

        u, v = pairs(0, 2), pairs(1, 3)
        w = [
            v[0],
            ((v[1][0] - v[1][1]) * ROOT_HALF, (v[1][0] + v[1][1]) * ROOT_HALF),
            (-v[2][1], v[2][0]),
            (-(v[3][0] + v[3][1]) * ROOT_HALF, (v[3][0] - v[3][1]) * ROOT_HALF),
        ]
        return u, w

    def fold_in(h):
        def transpose(n):
            p, jb = n // 2, lax.rem(n, 2)
            for part in range(2):
                y = [recvf[h, p * GQ + jb * 4 + g, part] for g in range(4)]
                xt[p, part, jb] = jnp.concatenate(y, axis=0).T

        loop(2 * QUARTER, transpose)

        def body(n):
            jb, i = n // (LANES // RB), lax.rem(n, LANES // RB)
            rows = pl.ds(pl.multiple_of(i * RB, RB), RB)
            low_rows = pl.ds(pl.multiple_of(LANES + i * RB, RB), RB)
            re = [xt[p, 0, jb, rows, :] for p in range(QUARTER)]
            im = [xt[p, 1, jb, rows, :] for p in range(QUARTER)]

            u, w = turned(re, im)
            for s in range(4):
                for part in range(2):
                    cols = pl.ds(pl.multiple_of(part * 2 * LANES + jb * LANES, LANES), LANES)
                    for ss, y in ((s, u[s][part] + w[s][part]), (s + 4, u[s][part] - w[s][part])):
                        bx[ss, rows, cols], bx[ss, low_rows, cols] = split(y)

        loop(2 * LANES // RB, body)
        for jb in range(2):
            re, im = [], []
            for p in range(QUARTER):
                total = blank
                for g in range(4):
                    y = rim_r[p * GQ + jb * 4 + g]
                    y = jnp.where(odd_x, pltpu.roll(y, LANES // 2, 1), y)
                    total = jnp.where(lane8 // KHERE == g, rolled(y, KHERE * (g - h)), total)
                re.append(total)
                im.append(jnp.concatenate([total[TAPS:], total[:TAPS]], axis=0))
            u, w = turned(re, im)
            for s in range(4):
                for part in range(2):
                    cols = slice((2 * part + jb) * LANES, (2 * part + jb + 1) * LANES)
                    rim_store(bx, s, cols, u[s][part] + w[s][part])
                    rim_store(bx, s + 4, cols, u[s][part] - w[s][part])

    def to_samples():
        def body(s):
            y, rim = quadrants(jnp.dot(bx[s], tf[s], preferred_element_type=F32))
            for half in range(2):
                cols = slice(half * LANES, (half + 1) * LANES)
                sm[2 * s + half, 8 : 8 + LANES, :] = y[:, cols]
                sm[2 * s + half, 8 - TAPS : 8, :] = rim[:TAPS, cols] * keep_down

        loop(RADIX, body)

    def make_stream(acc):
        def body(n, acc):
            w = [win[k, n] for k in range(TAPS)]
            for i in range(LANES // 8):
                total = w[0] * sm[n, 8 + 8 * i : 16 + 8 * i, :]
                for k in range(1, TAPS):
                    total = total + w[k] * sm[n, 8 + 8 * i - k : 16 + 8 * i - k, :]
                y = noise[n, 8 * i : 8 * i + 8, :] * total
                st[n, 8 * i + 8 : 8 * i + 16, :] = y
                acc = acc + y * total
            return acc

        return loop(TILES, body, acc)

    def make_weighted():
        def body(s):
            for half in range(2):
                n = 2 * s + half
                cols = slice(half * LANES, (half + 1) * LANES)
                w = [jnp.concatenate([win[k, n]] * (RB // 8), axis=0) for k in range(TAPS)]
                for i in range(LANES // RB):
                    total = w[0] * st[n, 8 + RB * i : 8 + RB * (i + 1), :]
                    for k in range(1, TAPS):
                        total = total + w[k] * st[n, 8 + RB * i + k : 8 + RB * (i + 1) + k, :]
                    high, low = split(total)
                    bw[s, RB * i : RB * (i + 1), cols] = high
                    bw[s, LANES + RB * i : LANES + RB * (i + 1), cols] = low
                rim = win[0, n] * st[n, 0:8, :]
                for k in range(1, TAPS):
                    rim = rim + win[k, n] * st[n, k : 8 + k, :]
                rim_store(bw, s, cols, rim)

        loop(RADIX, body)

    def to_spectra():
        def body(s):
            y, rim = quadrants(jnp.dot(bw[s], tb[s], preferred_element_type=F32))
            vv[s, :LANES, :] = y
            vv[s, LANES:, :] = rim

        loop(RADIX, body)

    def joined_image(re, im):
        ar = [re[s] + re[s + 4] for s in range(4)]
        ai = [im[s] + im[s + 4] for s in range(4)]
        dr = [re[s] - re[s + 4] for s in range(4)]
        di = [im[s] - im[s + 4] for s in range(4)]
        one = ((dr[1] + di[1]) * ROOT_HALF, (di[1] - dr[1]) * ROOT_HALF)
        one3 = ((di[1] - dr[1]) * ROOT_HALF, -(di[1] + dr[1]) * ROOT_HALF)
        three = ((di[3] - dr[3]) * ROOT_HALF, -(di[3] + dr[3]) * ROOT_HALF)
        three3 = ((dr[3] + di[3]) * ROOT_HALF, (di[3] - dr[3]) * ROOT_HALF)
        return [
            ((ar[0] + ar[2]) + (ar[1] + ar[3]), (ai[0] + ai[2]) + (ai[1] + ai[3])),
            ((dr[0] + di[2]) + (one[0] + three[0]), (di[0] - dr[2]) + (one[1] + three[1])),
            ((ar[0] - ar[2]) + (ai[1] - ai[3]), (ai[0] - ai[2]) + (ar[3] - ar[1])),
            ((dr[0] - di[2]) + (one3[0] + three3[0]), (di[0] + dr[2]) + (one3[1] + three3[1])),
        ]

    def fold_out(h):
        def body(n):
            jb, i = n // (LANES // RB), lax.rem(n, LANES // RB)
            rows = pl.ds(pl.multiple_of(i * RB, RB), RB)
            cols = [pl.ds(pl.multiple_of((2 * part + jb) * LANES, LANES), LANES) for part in range(2)]
            re = [vv[s, rows, cols[0]] for s in range(RADIX)]
            im = [vv[s, rows, cols[1]] for s in range(RADIX)]
            image = joined_image(re, im)
            for p in range(QUARTER):
                for part in range(2):
                    xt[p, part, jb, rows, :] = image[p][part]

        loop(2 * LANES // RB, body)

        for jb in range(2):
            cols = [slice((2 * part + jb) * LANES, (2 * part + jb + 1) * LANES) for part in range(2)]
            image = joined_image(*[[vv[s, LANES:, cols[part]] for s in range(RADIX)] for part in range(2)])
            for p in range(QUARTER):
                rim_v[h, p, jb] = jnp.concatenate([image[p][0][TAPS:], image[p][1][TAPS:]], axis=0)

        def transpose(n):
            p, jb = n // 2, lax.rem(n, 2)
            for part in range(2):
                y = xt[p, part, jb].T
                for g in range(4):
                    sendb[h, p * GQ + jb * 4 + g, part] = y[KHERE * g : KHERE * (g + 1), :]

        loop(2 * QUARTER, transpose)

    def tm_copy(rnd, i):
        d = lax.rem(t + i + 1, SEGMENTS)
        return copy_to(part_t.at[rnd, t], part_t.at[rnd, t], ts.at[rnd], tr.at[rnd], (c, d))

    def tm_all(rnd):
        some = part_t.at[rnd, pl.ds(0, SEGMENTS - 1)]
        return copy_to(some, some, ts.at[rnd], tr.at[rnd], some_dev)

    def chan_copy(rnd, i):
        d = lax.rem(c + i + 1, GROUPS)
        return copy_to(part_c.at[rnd, c], part_c.at[rnd, c], cs.at[rnd], cr.at[rnd], (d, t))

    def chan_all(rnd):
        some = part_c.at[rnd, pl.ds(0, GROUPS - 1)]
        return copy_to(some, some, cs.at[rnd], cr.at[rnd], some_dev)

    def sum_start(rnd, row):
        part_t[rnd, t] = row
        loop(SEGMENTS - 1, lambda i: tm_copy(rnd, i).start())

    def sum_middle(rnd):
        tm_all(rnd).wait_recv()
        part_c[rnd, c] = jnp.sum(part_t[rnd], axis=0)
        loop(GROUPS - 1, lambda i: chan_copy(rnd, i).start())

    def sum_end(rnd):
        chan_all(rnd).wait_recv()
        return jnp.sum(part_c[rnd], axis=0)

    def sum_sent(rnd):
        tm_all(rnd).wait_send()
        chan_all(rnd).wait_send()

    lane_row = lax.broadcasted_iota(jnp.int32, (1, LANES), 1)

    def both(first, second):
        a = jnp.sum(first, axis=0, keepdims=True)
        b = jnp.sum(second, axis=0, keepdims=True)
        half = LANES // 2
        return jnp.where(lane_row < half, a + pltpu.roll(a, half, 1), b + pltpu.roll(b, half, 1))

    curve = jnp.zeros((8, LANES), F32)
    for h in range(HALF):
        self_f[h].wait()
        forward_all(h).wait_recv()
        if h == 0:
            rim_wait(0, False)
        fold_in(h)
        to_samples()
        curve = make_stream(curve)
        if h == HALF - 1:
            sum_start(0, both(norm_part, curve))
        make_weighted()
        to_spectra()
        fold_out(h)
        if h == HALF - 1:
            sum_middle(0)
            for n in range(GROUPS):
                p, jb, g = n // 8, (n // 4) % 2, n % 4
                first, second = rolled(rim_v[0, p, jb], -KHERE * g), rolled(rim_v[1, p, jb], KHERE - KHERE * g)
                back_s[n] = jnp.where(lane8 < KHERE, first, second)
            rim_start(rim_back)
        loop(GROUPS - 1, lambda i: backward_copy(h, i).start())
        self_b[h].start()

    sums = sum_end(0)
    zero = jnp.zeros((1, LANES), F32)
    norm_now = jnp.sum(jnp.where(lane_row < LANES // 2, sums, zero), axis=1, keepdims=True)
    alpha = norm_now / jnp.sum(jnp.where(lane_row < LANES // 2, zero, sums), axis=1, keepdims=True)

    def step_solution(i):
        part, f = i // FEEDS, lax.rem(i, FEEDS)
        nsol[part, f] = nsol[part, f] + alpha * dirv[part, f]

    loop(2 * FEEDS, step_solution)

    rim_wait(1, False)

    def take_rim(zz):
        above = lax.rem(zz + 1, ROWS_Z) * ACROSS
        keep = jnp.where((zz == ROWS_Z - 1) & (t == SEGMENTS - 1), 0.0, 1.0).astype(F32)
        for h in range(HALF):
            total = blank
            for xx in range(ACROSS):
                total = jnp.where(lane8 // KHERE == xx, rolled(back_r[above + xx], KHERE * (xx - h)), total)
            total = total * (keep * alpha)
            for part in range(2):
                last = total[TAPS * part : TAPS * (part + 1)]
                y = jnp.concatenate([jnp.zeros((LANES - TAPS, LANES), F32), last], axis=0).T
                for xx in range(ACROSS):
                    f = HALF * xx + h
                    nres[part, f, :, frames_of(zz)] = (
                        nres[part, f, :, frames_of(zz)] - y[KHERE * xx : KHERE * (xx + 1), :]
                    )

    loop(ROWS_Z, take_rim)

    norm_next = jnp.zeros((8, LANES), F32)
    for h in range(HALF):
        self_b[h].wait()
        backward_all(h).wait_recv()

        def update(i, acc):
            part, f = i // ACROSS, HALF * lax.rem(i, ACROSS) + h
            y = nres[part, f] - alpha * recvb[part, f]
            nres[part, f] = y
            return acc + fold_rows(y * y)

        norm_next = loop(2 * ACROSS, update, norm_next)

    sum_start(1, jnp.sum(norm_next, axis=0, keepdims=True))
    sum_middle(1)
    total = jnp.sum(sum_end(1), axis=1, keepdims=True)
    beta_ref[...] = jnp.broadcast_to(total / norm_now, (8, LANES))
    for h in range(HALF):
        forward_all(h).wait_send()
        backward_all(h).wait_send()
    noise_all().wait_send()
    rim_wait(0, True)
    rim_wait(1, True)
    sum_sent(0)
    sum_sent(1)


def finish_kernel(nsol, nres, dirv, beta_ref, sol_out, res_out, dir_out, ndir, sem):
    copies = [
        pltpu.make_async_copy(nsol, sol_out, sem.at[0]),
        pltpu.make_async_copy(nres, res_out, sem.at[1]),
    ]
    for cp in copies:
        cp.start()
    beta = beta_ref[0:1, 0:1]
    for part in range(2):
        def body(f):
            ndir[part, f] = nres[part, f] + beta * dirv[part, f]

        loop(FEEDS, body)
        cp = pltpu.make_async_copy(ndir.at[part], dir_out.at[part], sem.at[2 + part])
        cp.start()
        copies.append(cp)
    for cp in copies:
        cp.wait()


def per_device(solution_, residual, direction, sample_weight):
    forward, backward = tables()
    window = window_table()
    shape = direction.shape
    vmem = pl.BlockSpec(memory_space=pltpu.VMEM)
    hbm = pl.BlockSpec(memory_space=pl.ANY)
    dma = pltpu.SemaphoreType.DMA
    piece = (2, KHERE, LANES)
    nsol, nres, dirv, beta = pl.pallas_call(
        exchange_kernel,
        name="exchange",
        out_shape=[pltpu.VMEM(shape, F32)] * 3 + [pltpu.VMEM((8, LANES), F32)],
        in_specs=[hbm] * 7,
        out_specs=[vmem] * 4,
        scratch_shapes=[
            pltpu.VMEM((HALF, GROUPS) + piece, F32),
            pltpu.VMEM((HALF, GROUPS) + piece, F32),
            pltpu.VMEM(shape, F32),
            pltpu.VMEM((ROWS_Z, 2, 8, LANES), F32),
            pltpu.VMEM((GROUPS, 8, LANES), F32),
            pltpu.VMEM((GROUPS, 8, LANES), F32),
            pltpu.VMEM((GROUPS, 8, LANES), F32),
            pltpu.VMEM((HALF, QUARTER, 2, 8, LANES), F32),
            pltpu.VMEM(forward.shape, BF16),
            pltpu.VMEM(backward.shape, BF16),
            pltpu.VMEM(window.shape, F32),
            pltpu.VMEM((ACROSS, BLOCK, SAMPLES), F32),
            pltpu.VMEM((SAMPLES, LANES), F32),
            pltpu.VMEM((TILES, LANES, LANES), F32),
            pltpu.VMEM((QUARTER, 2, 2, LANES, LANES), F32),
            pltpu.VMEM((RADIX, STACK, INNER), BF16),
            pltpu.VMEM((TILES, LANES + 8, LANES), F32),
            pltpu.VMEM((TILES, LANES + 16, LANES), F32),
            pltpu.VMEM((RADIX, STACK, ROWS), BF16),
            pltpu.VMEM((RADIX, LANES + 8, INNER), F32),
            pltpu.VMEM((2, GROUPS, 1, LANES), F32),
            pltpu.VMEM((2, SEGMENTS, 1, LANES), F32),
            dma((7,)),
            dma((3, HALF)),
            dma((HALF,)),
            dma((HALF,)),
            dma((HALF,)),
            dma((HALF,)),
            dma((2,)),
            dma((2,)),
            dma((1,)),
            dma((1,)),
            dma((2,)),
            dma((2,)),
            dma((2,)),
            dma((2,)),
        ],
        compiler_params=pltpu.CompilerParams(
            collective_id=0, has_side_effects=True, vmem_limit_bytes=52 * 2**20
        ),
    )(solution_, residual, direction, sample_weight, forward, backward, window)
    inside = [pltpu.with_memory_space_constraint(x, pltpu.VMEM) for x in (nsol, nres, dirv, beta)]
    return pl.pallas_call(
        finish_kernel,
        name="finish",
        out_shape=[jax.ShapeDtypeStruct(shape, F32)] * 3,
        in_specs=[vmem] * 4,
        out_specs=[hbm] * 3,
        scratch_shapes=[pltpu.VMEM(shape, F32), dma((4,))],
        compiler_params=pltpu.CompilerParams(vmem_limit_bytes=24 * 2**20),
    )(*inside)


def solution(mesh):
    placed = P(None, None, "chan", "tm")
    return jax.shard_map(
        per_device,
        mesh=mesh,
        in_specs=(placed, placed, placed, P("tm", "chan", None, None)),
        out_specs=(placed, placed, placed),
        check_vma=False,
    )
```

time: 160 us -> 126 us (0.79)
  Pallas kernels: 159 us -> 126 us
    pallas_call x1, Pallas kernels: 156 us -> 123 us  [per_device(): pl.pallas_call(exchange_kernel, name='exchange', out_shape=[pltpu.VMEM(sh...]
where the time goes in v2:
time: 126 us
  Pallas kernels  126 us (100%)
    pallas_call x1, Pallas kernels, per_device(): pl.pallas_call(exchange_kernel, name='exchange', out_shape=[pltpu.VMEM(sh...  123 us
    pallas_call x1, Pallas kernels, per_device(): pl.pallas_call(finish_kernel, name='finish', out_shape=[jax.ShapeDtypeStr...  2.7 us

profile of v2, /device:TPU:1, one launch (start us, length us, event | category | flops | bytes accessed | tf_op | source)
XLA Modules:
  0.0 126.3 jit_solution(6610781623426866828)
XLA Ops:
  0.6 122.9 %exchange.1 = (f32[2,8,32,1024]{3,2,1,0:T(8,128)S(1)}, f32[2,8,32,1024]{3,2,1,0:T(8,128)S(1)}, f32[2,8,32,1024]{3,2,1,0:T(8,128)S(1)}, f32[8,128]{1,0:T(8,128)S(1)}) custom-call(f32[2,8,32,1024]{3,2,1,0:T(8,128)} %sol_hbm.1, f32[2,8,32,1024]{3,2,1,0:T(8,128)} %res_hbm.1, f32[2,8,32,1024]{3,2,1,0:T(8,128)} %dir_hbm.1, f32[1,1,32,2048]{3,2,1,0:T(8,128)} %wgt_hbm.1, ...), custom_call_target="tpu_custom_call" | custom-call | tf_op jit(solution)/shard_map/exchange/pallas_call | solution.py:618
  123.6 2.7 %finish.1 = (f32[2,8,32,1024]{3,2,1,0:T(8,128)}, f32[2,8,32,1024]{3,2,1,0:T(8,128)}, f32[2,8,32,1024]{3,2,1,0:T(8,128)}) custom-call(f32[2,8,32,1024]{3,2,1,0:T(8,128)S(1)} %get-tuple-element.7.nsol, f32[2,8,32,1024]{3,2,1,0:T(8,128)S(1)} %get-tuple-element.8.nres, f32[2,8,32,1024]{3,2,1,0:T(8,128)S(1)} %get-tuple-element.9.dirv, ...), custom_call_target="tpu_custom_call" | custom-call | tf_op jit(solution)/shard_map/finish/pallas_call | solution.py:667

commit v3 on v2

--- a/solution.py
+++ b/solution.py
@@ -180,7 +180,7 @@
         zz, xx = n // ACROSS, lax.rem(n, ACROSS)
         cc = lax.rem((zz + 1) * ACROSS + xx, GROUPS)
         tt = jnp.where(zz == ROWS_Z - 1, t_up, t)
-        src = rim_s.at[zz, xx // 2]
+        src = rim_s.at[zz, xx]
         remote = copy_to(src, rim_r.at[c], rim_sent.at[0], rim_got.at[0], (cc, tt))
         return (zz + 1) * ACROSS + xx == c, remote, pltpu.make_async_copy(src, rim_r.at[c], self_sem.at[2, 0])
 
@@ -241,11 +241,16 @@
     pl.semaphore_wait(barrier, PEERS + SEGMENTS - 1 + ACROSS + jnp.where(z == 0, GROUPS, 0))
     loop(GROUPS - 1, lambda i: forward_copy(0, i).start())
 
+    low8 = lax.broadcasted_iota(jnp.int32, (8, LANES), 1) < LANES // 2
+
     def pack_rim(n):
         zz, fh = n // 2, lax.rem(n, 2)
-        for part in range(2):
-            y = jnp.concatenate([dirv[part, 4 * fh + f, :, frames_of(zz)] for f in range(4)], axis=0).T
-            rim_s[zz, fh, TAPS * part : TAPS * (part + 1), :] = y[LANES - TAPS :, :]
+        y = [
+            jnp.concatenate([dirv[part, 4 * fh + f, :, frames_of(zz)] for f in range(4)], axis=0).T[LANES - 8 :]
+            for part in range(2)
+        ]
+        rim_s[zz, 2 * fh] = jnp.where(low8, y[0], pltpu.roll(y[1], LANES // 2, 1))[TAPS:]
+        rim_s[zz, 2 * fh + 1] = jnp.where(low8, pltpu.roll(y[0], LANES // 2, 1), y[1])[TAPS:]
 
     loop(2 * ROWS_Z, pack_rim)
     rim_start(rim_to)
@@ -299,7 +304,6 @@
         ref[s, MAIN + RIM : STACK, cols] = low
 
     lane8 = lax.broadcasted_iota(jnp.int32, (8, LANES), 1)
-    odd_x = jnp.full((8, LANES), lax.rem(x_here, 2), jnp.int32) == 1
 
     def rolled(x, by):
         by = by % LANES
@@ -352,13 +356,15 @@
         for jb in range(2):
             re, im = [], []
             for p in range(QUARTER):
-                total = blank
+                both_parts = [blank, blank]
                 for g in range(4):
                     y = rim_r[p * GQ + jb * 4 + g]
-                    y = jnp.where(odd_x, pltpu.roll(y, LANES // 2, 1), y)
-                    total = jnp.where(lane8 // KHERE == g, rolled(y, KHERE * (g - h)), total)
-                re.append(total)
-                im.append(jnp.concatenate([total[TAPS:], total[:TAPS]], axis=0))
+                    y = jnp.concatenate([y, y], axis=0)
+                    for part in range(2):
+                        moved = rolled(y, KHERE * (g - h - 2 * part))
+                        both_parts[part] = jnp.where(lane8 // KHERE == g, moved, both_parts[part])
+                re.append(both_parts[0])
+                im.append(both_parts[1])
             u, w = turned(re, im)
             for s in range(4):
                 for part in range(2):
@@ -523,7 +529,9 @@
             for n in range(GROUPS):
                 p, jb, g = n // 8, (n // 4) % 2, n % 4
                 first, second = rolled(rim_v[0, p, jb], -KHERE * g), rolled(rim_v[1, p, jb], KHERE - KHERE * g)
-                back_s[n] = jnp.where(lane8 < KHERE, first, second)
+                y = jnp.where(lane8 < KHERE, first, second)
+                other = jnp.concatenate([y[TAPS:], y[:TAPS]], axis=0)
+                back_s[n] = jnp.where(low8, y, pltpu.roll(other, LANES // 2, 1))[:TAPS]
             rim_start(rim_back)
         loop(GROUPS - 1, lambda i: backward_copy(h, i).start())
         self_b[h].start()
@@ -541,17 +549,20 @@
 
     rim_wait(1, False)
 
+    last8 = lax.broadcasted_iota(jnp.int32, (8, LANES), 0) >= TAPS
+
     def take_rim(zz):
         above = lax.rem(zz + 1, ROWS_Z) * ACROSS
         keep = jnp.where((zz == ROWS_Z - 1) & (t == SEGMENTS - 1), 0.0, 1.0).astype(F32)
         for h in range(HALF):
-            total = blank
-            for xx in range(ACROSS):
-                total = jnp.where(lane8 // KHERE == xx, rolled(back_r[above + xx], KHERE * (xx - h)), total)
-            total = total * (keep * alpha)
             for part in range(2):
-                last = total[TAPS * part : TAPS * (part + 1)]
-                y = jnp.concatenate([jnp.zeros((LANES - TAPS, LANES), F32), last], axis=0).T
+                total = jnp.zeros((8, LANES), F32)
+                for xx in range(ACROSS):
+                    y = back_r[above + xx]
+                    y = rolled(jnp.concatenate([y, y], axis=0), KHERE * (xx - h - 2 * part))
+                    total = jnp.where((lane8 // KHERE == xx) & last8, y, total)
+                total = total * (keep * alpha)
+                y = jnp.concatenate([jnp.zeros((LANES - 8, LANES), F32), total], axis=0).T
                 for xx in range(ACROSS):
                     f = HALF * xx + h
                     nres[part, f, :, frames_of(zz)] = (
@@ -625,10 +636,10 @@
             pltpu.VMEM((HALF, GROUPS) + piece, F32),
             pltpu.VMEM((HALF, GROUPS) + piece, F32),
             pltpu.VMEM(shape, F32),
-            pltpu.VMEM((ROWS_Z, 2, 8, LANES), F32),
-            pltpu.VMEM((GROUPS, 8, LANES), F32),
-            pltpu.VMEM((GROUPS, 8, LANES), F32),
-            pltpu.VMEM((GROUPS, 8, LANES), F32),
+            pltpu.VMEM((ROWS_Z, ACROSS, TAPS, LANES), F32),
+            pltpu.VMEM((GROUPS, TAPS, LANES), F32),
+            pltpu.VMEM((GROUPS, TAPS, LANES), F32),
+            pltpu.VMEM((GROUPS, TAPS, LANES), F32),
             pltpu.VMEM((HALF, QUARTER, 2, 8, LANES), F32),
             pltpu.VMEM(forward.shape, BF16),
             pltpu.VMEM(backward.shape, BF16),

time: 126 us -> 124 us (0.984)
  Pallas kernels: 126 us -> 123 us
    pallas_call x1, Pallas kernels: 123 us -> 120 us  [per_device(): pl.pallas_call(exchange_kernel, name='exchange', out_shape=[pltpu.VMEM(sh...]
where the time goes in v3:
time: 124 us; the launch traced here: 123 us
  Pallas kernels  123 us (99%)
    pallas_call x1, Pallas kernels, per_device(): pl.pallas_call(exchange_kernel, name='exchange', out_shape=[pltpu.VMEM(sh...  120 us
    pallas_call x1, Pallas kernels, per_device(): pl.pallas_call(finish_kernel, name='finish', out_shape=[jax.ShapeDtypeStr...  2.7 us

profile of v3, /device:TPU:1, one launch (start us, length us, event | category | flops | bytes accessed | tf_op | source)
XLA Modules:
  0.0 123.5 jit_solution(15543274062590084422)
XLA Ops:
  0.6 120.1 %exchange.1 = (f32[2,8,32,1024]{3,2,1,0:T(8,128)S(1)}, f32[2,8,32,1024]{3,2,1,0:T(8,128)S(1)}, f32[2,8,32,1024]{3,2,1,0:T(8,128)S(1)}, f32[8,128]{1,0:T(8,128)S(1)}) custom-call(f32[2,8,32,1024]{3,2,1,0:T(8,128)} %sol_hbm.1, f32[2,8,32,1024]{3,2,1,0:T(8,128)} %res_hbm.1, f32[2,8,32,1024]{3,2,1,0:T(8,128)} %dir_hbm.1, f32[1,1,32,2048]{3,2,1,0:T(8,128)} %wgt_hbm.1, ...), custom_call_target="tpu_custom_call" | custom-call | tf_op jit(solution)/shard_map/exchange/pallas_call | solution.py:629
  120.8 2.7 %finish.1 = (f32[2,8,32,1024]{3,2,1,0:T(8,128)}, f32[2,8,32,1024]{3,2,1,0:T(8,128)}, f32[2,8,32,1024]{3,2,1,0:T(8,128)}) custom-call(f32[2,8,32,1024]{3,2,1,0:T(8,128)S(1)} %get-tuple-element.7.nsol, f32[2,8,32,1024]{3,2,1,0:T(8,128)S(1)} %get-tuple-element.8.nres, f32[2,8,32,1024]{3,2,1,0:T(8,128)S(1)} %get-tuple-element.9.dirv, ...), custom_call_target="tpu_custom_call" | custom-call | tf_op jit(solution)/shard_map/finish/pallas_call | solution.py:678

commit v4 on v3

--- a/solution.py
+++ b/solution.py
@@ -159,8 +159,13 @@
         some = recvf.at[h, pl.ds(0, GROUPS - 1)]
         return copy_to(some, some, fs.at[h], fr.at[h], some_dev)
 
+    def spread(i):
+        i = PEERS - 1 - i
+        e, odd = i // 2, lax.rem(i, 2)
+        return lax.rem(c + (1 + e) * (1 - odd) + (PEERS - e) * odd, GROUPS)
+
     def backward_copy(h, i):
-        d = lax.rem(c + i + 1, GROUPS)
+        d = spread(i)
         dst = recvb.at[:, HALF * x_here + h, :, frames_of(z)]
         return copy_to(sendb.at[h, d], dst, bs.at[h], br.at[h], (d, t))
 

time: 124 us -> 120 us (0.968)
  Pallas kernels: 123 us -> 120 us
    pallas_call x1, Pallas kernels: 120 us -> 117 us  [per_device(): pl.pallas_call(exchange_kernel, name='exchange', out_shape=[pltpu.VMEM(sh...]
where the time goes in v4:
time: 120 us
  Pallas kernels  120 us (100%)
    pallas_call x1, Pallas kernels, per_device(): pl.pallas_call(exchange_kernel, name='exchange', out_shape=[pltpu.VMEM(sh...  117 us
    pallas_call x1, Pallas kernels, per_device(): pl.pallas_call(finish_kernel, name='finish', out_shape=[jax.ShapeDtypeStr...  2.7 us

profile of v4, /device:TPU:1, one launch (start us, length us, event | category | flops | bytes accessed | tf_op | source)
XLA Modules:
  0.0 120.3 jit_solution(13540483343751155122)
XLA Ops:
  0.6 117.0 %exchange.1 = (f32[2,8,32,1024]{3,2,1,0:T(8,128)S(1)}, f32[2,8,32,1024]{3,2,1,0:T(8,128)S(1)}, f32[2,8,32,1024]{3,2,1,0:T(8,128)S(1)}, f32[8,128]{1,0:T(8,128)S(1)}) custom-call(f32[2,8,32,1024]{3,2,1,0:T(8,128)} %sol_hbm.1, f32[2,8,32,1024]{3,2,1,0:T(8,128)} %res_hbm.1, f32[2,8,32,1024]{3,2,1,0:T(8,128)} %dir_hbm.1, f32[1,1,32,2048]{3,2,1,0:T(8,128)} %wgt_hbm.1, ...), custom_call_target="tpu_custom_call" | custom-call | tf_op jit(solution)/shard_map/exchange/pallas_call | solution.py:634
  117.6 2.7 %finish.1 = (f32[2,8,32,1024]{3,2,1,0:T(8,128)}, f32[2,8,32,1024]{3,2,1,0:T(8,128)}, f32[2,8,32,1024]{3,2,1,0:T(8,128)}) custom-call(f32[2,8,32,1024]{3,2,1,0:T(8,128)S(1)} %get-tuple-element.7.nsol, f32[2,8,32,1024]{3,2,1,0:T(8,128)S(1)} %get-tuple-element.8.nres, f32[2,8,32,1024]{3,2,1,0:T(8,128)S(1)} %get-tuple-element.9.dirv, ...), custom_call_target="tpu_custom_call" | custom-call | tf_op jit(solution)/shard_map/finish/pallas_call | solution.py:683

commit v5 on v4

--- a/solution.py
+++ b/solution.py
@@ -130,7 +130,7 @@
             )
         )
     ]
-    for cp in loads:
+    for cp in loads[:2]:
         cp.start()
     loop(GROUPS - 1, greet_chan)
     loop(SEGMENTS - 1, greet_tm)
@@ -245,6 +245,8 @@
         self_f[h].start()
     pl.semaphore_wait(barrier, PEERS + SEGMENTS - 1 + ACROSS + jnp.where(z == 0, GROUPS, 0))
     loop(GROUPS - 1, lambda i: forward_copy(0, i).start())
+    for cp in loads[2:]:
+        cp.start()
 
     low8 = lax.broadcasted_iota(jnp.int32, (8, LANES), 1) < LANES // 2
 

time: 120 us -> 120 us (level)
  no operation moved by 1% of the time
where the time goes in v5:
time: 120 us
  Pallas kernels  120 us (100%)
    pallas_call x1, Pallas kernels, per_device(): pl.pallas_call(exchange_kernel, name='exchange', out_shape=[pltpu.VMEM(sh...  117 us
    pallas_call x1, Pallas kernels, per_device(): pl.pallas_call(finish_kernel, name='finish', out_shape=[jax.ShapeDtypeStr...  2.7 us

profile of v5, /device:TPU:1, one launch (start us, length us, event | category | flops | bytes accessed | tf_op | source)
XLA Modules:
  0.0 120.3 jit_solution(11578750130710419376)
XLA Ops:
  0.6 117.0 %exchange.1 = (f32[2,8,32,1024]{3,2,1,0:T(8,128)S(1)}, f32[2,8,32,1024]{3,2,1,0:T(8,128)S(1)}, f32[2,8,32,1024]{3,2,1,0:T(8,128)S(1)}, f32[8,128]{1,0:T(8,128)S(1)}) custom-call(f32[2,8,32,1024]{3,2,1,0:T(8,128)} %sol_hbm.1, f32[2,8,32,1024]{3,2,1,0:T(8,128)} %res_hbm.1, f32[2,8,32,1024]{3,2,1,0:T(8,128)} %dir_hbm.1, f32[1,1,32,2048]{3,2,1,0:T(8,128)} %wgt_hbm.1, ...), custom_call_target="tpu_custom_call" | custom-call | tf_op jit(solution)/shard_map/exchange/pallas_call | solution.py:636
  117.6 2.7 %finish.1 = (f32[2,8,32,1024]{3,2,1,0:T(8,128)}, f32[2,8,32,1024]{3,2,1,0:T(8,128)}, f32[2,8,32,1024]{3,2,1,0:T(8,128)}) custom-call(f32[2,8,32,1024]{3,2,1,0:T(8,128)S(1)} %get-tuple-element.7.nsol, f32[2,8,32,1024]{3,2,1,0:T(8,128)S(1)} %get-tuple-element.8.nres, f32[2,8,32,1024]{3,2,1,0:T(8,128)S(1)} %get-tuple-element.9.dirv, ...), custom_call_target="tpu_custom_call" | custom-call | tf_op jit(solution)/shard_map/finish/pallas_call | solution.py:685
